TPU v7x, 128 devices: a whole 4x4x4 slice. The times are simulated.
128 devices in a mesh: dp: 16 (over z, x_lo, core), mp: 8 (over x_hi, y).
Axes of the slice: x: 4 (x_hi: 2, x_lo: 2; x = x_hi * 2 + x_lo), y: 4, z: 4, core: 2. Of those that a mesh axis runs over, the one named last changes fastest.
Arguments:
- old_store: bfloat16 [4096, 4096], P('mp', 'dp'), may hold values from -0.09375 to 0.09375
- block_map: int32 [32], replicated, may hold values from 0 to 31, each once
- expand_in: bfloat16 [8192, 4096], P('mp', 'dp'), may hold values from -0.0625 to 0.0625
- expand_out: bfloat16 [8192, 4096], P('dp'), may hold values from -0.09375 to 0.09375
- attn: bfloat16 [4096, 8192], P('dp', 'mp'), may hold values from -6 to 6
- residual: bfloat16 [4096, 8192], P('dp', 'mp'), may hold values from -6 to 6
Outputs:
- stream: bfloat16 [4096, 8192], P('dp', 'mp')
Inputs may be any that keep to these rules, and one draw needn't show every extreme that they name: `block_map`: a permutation: every row block of the old weight is held by exactly one stored block.
All inputs are finite; a program needn't handle non-finite values.
Results may differ from a plain program's by a relative error of at most 0.023.
Values may be sent and summed in bfloat16 or wider, within the bound.
A program may use at most 128 MiB of HBM per device.

v0:
```python
import jax
import jax.numpy as jnp
from jax import lax
from jax.sharding import PartitionSpec as P

BLOCK = 128


def contract_last(left_side, right_side):
    return lax.dot_general(
        left_side, right_side, (((1,), (1,)), ((), ())), preferred_element_type=jnp.float32
    )


def shards(old_store, block_map, expand_in, expand_out, attn, residual):
    block_count = block_map.shape[0]
    block_rows = old_store.shape[1] * 0 + BLOCK
    stored_sum = contract_last(lax.all_gather(old_store, "mp", axis=0, tiled=True), expand_in)
    slot_ids = jnp.arange(block_count, dtype=jnp.int32)
    source = jnp.sum(
        jnp.where(block_map[None, :] == slot_ids[:, None], slot_ids[None, :], 0), axis=1
    )
    ordered = jnp.take(stored_sum.reshape(block_count, block_rows, -1), source, axis=0)
    ordered = ordered.reshape(block_count * block_rows, -1)
    right = lax.psum(ordered.astype(jnp.bfloat16), "dp")
    grown = jnp.dot(expand_out, right, preferred_element_type=jnp.float32).astype(jnp.bfloat16)
    products = contract_last(attn, lax.all_gather(grown, "dp", axis=0, tiled=True))
    summed = lax.psum_scatter(
        products.astype(jnp.bfloat16), "mp", scatter_dimension=1, tiled=True
    ).astype(jnp.float32)
    return (summed + residual.astype(jnp.float32)).astype(jnp.bfloat16)


def solution(mesh):
    placed = (P("mp", "dp"), P(), P("mp", "dp"), P("dp", None), P("dp", "mp"), P("dp", "mp"))
    return jax.shard_map(
        shards, mesh=mesh, in_specs=placed, out_specs=P("dp", "mp"), check_vma=False
    )
```

profile of v0, /device:TPU:6, one launch (start us, length us, event | category | flops | bytes accessed | tf_op | source)
XLA Modules:
  0.0 488.0 jit_solution(312746784003697472)
XLA Ops:
  6.5 0.0 copy-start
  6.5 0.0 all-gather.3.cloned.1.call-start
  6.5 0.7 all-gather.3.cloned.1.call-update
  7.3 0.0 all-reduce.2.cloned.1.call-start
  7.3 0.8 select_reduce_fusion
  8.1 0.1 broadcast_bitcast_fusion
  8.2 56.2 %all-gather.3.cloned.1.call-done = bf16[4096,256]{1,0:T(8,128)(2,1)} async-done(((bf16[512,256]{1,0:T(8,128)(2,1)}), bf16[4096,256]{1,0:T(8,128)(2,1)}) %all-gather.3.cloned.1.call-update) | async-done | bytes 2097168 | tf_op jit(solution)/shard_map/all_gather | solution.py:18
  64.4 0.0 copy-done
  64.4 7.2 %fusion.4 = bf16[4096,1024]{1,0:T(8,128)(2,1)} fusion(bf16[4096,256]{1,0:T(8,128)(2,1)} %all-gather.3.cloned.1.call-done, bf16[1024,256]{1,0:T(8,128)(2,1)S(1)} %copy-done), kind=kOutput, calls=%fused_computation.16 | convolution fusion | flops 2147483648 | bytes 11010048 | tf_op jit(solution)/shard_map/dot_general | solution.py:10
  71.6 8.4 %gather_fusion = bf16[32,128,1024]{2,1,0:T(8,128)(2,1)} fusion(bf16[32,128,1024]{2,1,0:T(8,128)(2,1)} %bitcast.21, s32[1024]{0:T(1024)S(1)} %pad_clamp_fusion), kind=kCustom, calls=%fused_computation | custom fusion | bytes 16777344 | tf_op jit(solution)/shard_map/jit(_take)/gather | solution.py:23
  80.0 7.6 %fusion = bf16[4096,1024]{1,0:T(8,128)(2,1)} fusion(bf16[32,128,1024]{2,1,0:T(8,128)(2,1)} %gather_fusion, pred[4096]{0:T(1024)(128)(4,1)S(1)} %broadcast_bitcast_fusion), kind=kLoop, calls=%fused_computation.2 | loop fusion | flops 4194304 | bytes 16781312 | tf_op jit(solution)/shard_map/convert_element_type | solution.py:25
  87.6 0.0 all-reduce.2.cloned.1.call-update
  87.6 0.0 copy-start.2
  87.6 0.0 all-gather.5.cloned.1.call-start
  87.7 191.0 %all-reduce.2.cloned.1.call-done = bf16[4096,1024]{1,0:T(8,128)(2,1)} async-done(((bf16[4096,1024]{1,0:T(8,128)(2,1)}), bf16[4096,1024]{1,0:T(8,128)(2,1)}) %all-reduce.2.cloned.1.call-update) | async-done | bytes 8388624 | tf_op jit(solution)/shard_map/psum | solution.py:25
  278.7 10.1 %fusion.2 = bf16[512,1024]{0,1:T(8,128)(2,1)} fusion(bf16[4096,1024]{1,0:T(8,128)(2,1)} %all-reduce.2.cloned.1.call-done, bf16[512,4096]{1,0:T(8,128)(2,1)} %param.9), kind=kOutput, calls=%fused_computation.6 | convolution fusion | flops 4295491584 | bytes 13631488 | tf_op jit(solution)/shard_map/dot_general | solution.py:26
  288.8 0.0 all-gather.5.cloned.1.call-update
  288.8 0.0 copy-start.1
  288.8 0.2 reduce-scatter.2.cloned.1.call-start
  289.0 93.5 %all-gather.5.cloned.1.call-done = bf16[8192,1024]{0,1:T(8,128)(2,1)} async-done(((bf16[512,1024]{0,1:T(8,128)(2,1)}), bf16[8192,1024]{0,1:T(8,128)(2,1)}) %all-gather.5.cloned.1.call-update) | async-done | bytes 16777232 | tf_op jit(solution)/shard_map/all_gather | solution.py:27
  382.6 0.0 copy-done.2
  382.6 12.5 %fusion.1 = bf16[256,8192]{0,1:T(8,128)(2,1)} fusion(bf16[8192,1024]{0,1:T(8,128)(2,1)} %all-gather.5.cloned.1.call-done, bf16[256,1024]{1,0:T(8,128)(2,1)S(1)} %copy-done.2), kind=kOutput, calls=%fused_computation.4 | convolution fusion | flops 4297064448 | bytes 21495808 | tf_op jit(solution)/shard_map/dot_general | solution.py:10
  395.1 0.0 reduce-scatter.2.cloned.1.call-update
  395.1 0.0 copy-done.1
  395.1 0.2 copy.9
  395.3 83.9 %reduce-scatter.2.cloned.1.call-done = bf16[256,1024]{0,1:T(8,128)(2,1)} async-done(((bf16[256,8192]{0,1:T(8,128)(2,1)}), bf16[256,1024]{0,1:T(8,128)(2,1)}) %reduce-scatter.2.cloned.1.call-update) | async-done | bytes 524304 | tf_op jit(solution)/shard_map/reduce_scatter | solution.py:28
  479.3 1.2 add_convert_fusion
  480.4 1.0 copy.10
  (3 shorter events, 0.0 us)
Async XLA Ops:
  6.5 57.9 %copy-start = (bf16[1024,256]{1,0:T(8,128)(2,1)S(1)}, bf16[1024,256]{1,0:T(8,128)(2,1)}, u32[]{:S(2)}) copy-start(bf16[1024,256]{1,0:T(8,128)(2,1)} %param.8) | copy-start | bytes 1572868
  6.5 57.9 %all-gather.3.cloned.1.call-start = ((), (), s32[]{:S(2)}) async-start(), calls=%async_computation.1 | async-start | bytes 2359296 | tf_op jit(solution)/shard_map/all_gather | solution.py:18
  7.3 271.4 %all-reduce.2.cloned.1.call-start = ((), (), s32[]{:S(2)}) async-start(), calls=%async_computation.2 | async-start | bytes 16777216 | tf_op jit(solution)/shard_map/psum | solution.py:25
  87.6 295.0 %copy-start.2 = (bf16[256,1024]{1,0:T(8,128)(2,1)S(1)}, bf16[256,1024]{1,0:T(8,128)(2,1)}, u32[]{:S(2)}) copy-start(bf16[256,1024]{1,0:T(8,128)(2,1)} %param.10) | copy-start | bytes 1572868
  87.6 294.9 %all-gather.5.cloned.1.call-start = ((), (), s32[]{:S(2)}) async-start(), calls=%async_computation.3 | async-start | bytes 17825792 | tf_op jit(solution)/shard_map/all_gather | solution.py:27
  288.8 106.3 %copy-start.1 = (bf16[256,1024]{1,0:T(8,128)(2,1)S(1)}, bf16[256,1024]{1,0:T(8,128)(2,1)}, u32[]{:S(2)}) copy-start(bf16[256,1024]{1,0:T(8,128)(2,1)} %param.11) | copy-start | bytes 1572868
  288.8 190.5 %reduce-scatter.2.cloned.1.call-start = ((), (), s32[]{:S(2)}) async-start(), calls=%async_computation.4 | async-start | bytes 4718592 | tf_op jit(solution)/shard_map/reduce_scatter | solution.py:28
Sparse Core Ops, SparseCore 0:
  9.7 54.6 all-gather.2
  87.7 190.8 all-reduce.1
  288.9 93.5 all-gather.4
  395.2 83.9 reduce-scatter.1
where the time goes:
time: 490 us; the launch traced here: 488 us
  waiting for transfers between devices  425 us (87%)
  matrix products  29.8 us (6%)
  between operations  13.2 us (3%)
  local copies, waits for them, and re-layouts  9.7 us (2%)
  other arithmetic  9.54 us (2%)
    psum x1, waiting for transfers between devices, shards(): right = lax.psum(ordered.astype(jnp.bfloat16), 'dp')  191 us
    all_gather x1, waiting for transfers between devices, shards(): lax.all_gather(grown, 'dp', axis=0, tiled=True)  93.5 us
    reduce_scatter x1, waiting for transfers between devices, shards(): lax.psum_scatter(products.astype(jnp.bfloat16), 'mp', scatter_dimension=1...  83.9 us
    all_gather x1, waiting for transfers between devices, shards(): lax.all_gather(old_store, 'mp', axis=0, tiled=True)  56.2 us
    dot_general x2, matrix products, contract_last(): lax.dot_general(left_side, right_side, (((1,), (1,)), ((), ())), preferre...  19.7 us
    dot_general x1, matrix products, shards(): jnp.dot(expand_out, right, preferred_element_type=jnp.float32)  10.1 us
  transfers between devices with their start and end apart: 4, of which 4 were waited for; matrix products, arithmetic and copies ran while one was open for 0% of the time, Pallas kernels for 0%

commit v1 on v0

v1 whole, which is shorter than its diff:
```python
import jax
import jax.numpy as jnp
from jax import lax
from jax.experimental import pallas as pl
from jax.experimental.pallas import tpu as pltpu
from jax.sharding import PartitionSpec as P

MESH = pl.DeviceIdType.MESH
BLOCK = 128
NCH = 2
F32 = jnp.float32
BF16 = jnp.bfloat16


def place(z, xl, c, xh, y):
    return {"dp": z * 4 + xl * 2 + c, "mp": xh * 4 + y}


def dot_nt(a, b):
    return lax.dot_general(a, b, (((1,), (1,)), ((), ())), preferred_element_type=F32)


def chain_kernel(
    map_ref, store_ref, ein_ref, eout_ref, attn_ref, out_ref,
    attn_g, ein_g, s_g, eo_raw, eo, p1, r1, ysum, xs, xr, a1g, p2, r2, a2g, ob,
    loc_sem, ein_ss, ein_rs, s_ss, s_rs, at_ss, at_rs, eo_ss, eo_rs, r1_ss, r1_rs, x_ss, x_rs,
    a1_ss, a1_rs, r2_ss, r2_rs, a2_ss, a2_rs, out_ss, out_rs,
):
    d = lax.axis_index("dp")
    m = lax.axis_index("mp")
    z, xl, c = d // 4, (d // 2) % 2, d % 2
    xh, y = m // 4, m % 4
    p = z * 2 + xl
    q0 = xl * 2 + c
    ox, oc, oh = 1 - xl, 1 - c, 1 - xh
    rows = attn_ref.shape[0] // NCH
    ry, rx = rows // 4, rows // 8
    sent = []

    def remote(src, dst, ss, rs, target):
        return pltpu.make_async_remote_copy(
            src_ref=src, dst_ref=dst, send_sem=ss, recv_sem=rs, device_id=target, device_id_type=MESH
        )

    def send(src, dst, ss, rs, target):
        copy = remote(src, dst, ss, rs, target)
        copy.start()
        sent.append(copy)

    def arrived(dst, ss, rs):
        remote(dst, dst, ss, rs, place(z, xl, oc, xh, y)).wait_recv()

    def zk(k):
        return lax.rem(z + k, 4)

    def yk(k):
        return lax.rem(y + k, 4)

    local = [
        pltpu.make_async_copy(attn_ref, attn_g.at[z], loc_sem.at[0]),
        pltpu.make_async_copy(ein_ref, ein_g.at[q0], loc_sem.at[1]),
        pltpu.make_async_copy(store_ref, s_g.at[q0, xh], loc_sem.at[2]),
    ]
    for copy in local:
        copy.start()

    @pl.loop(0, 32)
    def _(t):
        cols = pl.ds(pl.multiple_of(t * BLOCK, BLOCK), BLOCK)
        pltpu.make_async_copy(eout_ref.at[:, cols], eo_raw.at[t], loc_sem.at[3]).start()

    barrier = pltpu.get_barrier_semaphore()

    def greet(target):
        pl.semaphore_signal(barrier, inc=1, device_id=target, device_id_type=MESH)

    greet(place(z, xl, oc, xh, y))
    greet(place(z, ox, c, xh, y))
    greet(place(z, xl, c, oh, y))
    greet(place(z, ox, c, oh, y))
    for k in range(1, 4):
        greet(place(z, xl, c, xh, yk(k)))
        greet(place(zk(k), xl, c, xh, y))
        greet(place(zk(k), ox, c, xh, y))
        for l in range(1, 4):
            greet(place(zk(k), xl, c, xh, yk(l)))
    greeted = 4 + 3 * 6
    self_out = p == m
    for ms in range(8):
        @pl.when(jnp.logical_not(jnp.logical_and(self_out, m == ms)))
        def _():
            greet(place(m // 2, m % 2, c, ms // 4, ms % 4))
    pl.semaphore_wait(barrier, greeted + 8 - jnp.where(self_out, 1, 0))

    send(ein_ref, ein_g.at[q0], ein_ss.at[0], ein_rs.at[q0], place(z, xl, oc, xh, y))
    send(ein_ref, ein_g.at[q0], ein_ss.at[1], ein_rs.at[q0], place(z, ox, c, xh, y))
    for j in range(NCH):
        part = pl.ds(j * rows, rows)
        for k in (1, 3, 2):
            send(attn_ref.at[part], attn_g.at[z, part], at_ss.at[j, k], at_rs.at[j, z],
                 place(zk(k), xl, c, xh, y))
    mine = s_g.at[q0, xh]
    send(store_ref, mine, s_ss.at[0], s_rs.at[q0, xh], place(z, ox, c, xh, y))
    send(store_ref, mine, s_ss.at[1], s_rs.at[q0, xh], place(z, xl, c, oh, y))
    send(store_ref, mine, s_ss.at[2], s_rs.at[q0, xh], place(z, ox, c, oh, y))
    send(store_ref, mine, s_ss.at[3], s_rs.at[q0, xh], place(z, xl, oc, xh, y))

    pltpu.make_async_copy(eo_raw, eo_raw, loc_sem.at[3]).wait()

    @pl.loop(0, 32)
    def _(t):
        zs, ys, b = t // 8, (t // 2) % 4, t % 2
        s = ((zs // 2) * 4 + ys) * 4 + (zs % 2) * 2 + b
        eo[c, :, pl.ds(pl.multiple_of(t * BLOCK, BLOCK), BLOCK)] = eo_raw[map_ref[s]]

    send(eo.at[c], eo.at[c], eo_ss, eo_rs, place(z, xl, oc, xh, y))

    local[0].wait()
    local[1].wait()

    def multiply_in(j, q):
        lhs = attn_g[:, pl.ds(j * rows, rows), :].reshape(4 * rows, -1)
        res = jnp.dot(lhs, ein_g[q], preferred_element_type=F32).astype(BF16)
        res = res.reshape(4, 4, ry, 256)
        cols = pl.ds(pl.multiple_of(q * 256, 256), 256)
        for yt in range(4):
            p1[j, yt, :, :, cols] = res[:, yt]

    def half_cols(h):
        return pl.ds(pl.multiple_of(h * 512, 512), 512)

    def send_partials(j, hr):
        h = xl if hr == 0 else ox
        for k in (1, 3, 2):
            send(p1.at[j, yk(k), :, :, half_cols(h)], r1.at[j, hr, 3 - k], r1_ss.at[j, hr, k],
                 r1_rs.at[j, hr, 3 - k], place(z, xl, c, xh, yk(k)))

    for j in range(NCH):
        for k in (1, 3, 2):
            arrived(attn_g.at[zk(k), pl.ds(j * rows, rows)], at_ss.at[j, k], at_rs.at[j, zk(k)])
        for hr in range(2):
            qa = (xl if hr == 0 else ox) * 2 + c
            qb = (xl if hr == 0 else ox) * 2 + oc
            if j == 0:
                if hr == 1:
                    arrived(ein_g.at[qa], ein_ss.at[1], ein_rs.at[qa])
                    send(ein_g.at[qa], ein_g.at[qa], ein_ss.at[2], ein_rs.at[qa], place(z, xl, oc, xh, y))
            multiply_in(j, qa)
            if j == 0:
                arrived(ein_g.at[qb], ein_ss.at[0], ein_rs.at[qb])
            multiply_in(j, qb)
            send_partials(j, hr)

    local[2].wait()
    for i, (xls, xhs) in enumerate(((ox, xh), (xl, oh), (ox, oh))):
        qs = xls * 2 + c
        arrived(s_g.at[qs, xhs], s_ss.at[0], s_rs.at[qs, xhs])
        send(s_g.at[qs, xhs], s_g.at[qs, xhs], s_ss.at[4 + i], s_rs.at[qs, xhs], place(z, xl, oc, xh, y))

    def reduce_y(j, hr):
        h = xl if hr == 0 else ox
        cols = half_cols(h)
        for k in range(3):
            arrived(r1.at[j, hr, k], r1_ss.at[j, hr, 1], r1_rs.at[j, hr, k])

        @pl.loop(0, 4)
        def _(zs):
            total = p1[j, y, zs, :, cols].astype(F32)
            for k in range(3):
                total = total + r1[j, hr, k, zs].astype(F32)
            low, high = total[:rx], total[rx:]
            ysum[j, hr, zs] = jnp.where(xh == 0, low, high)
            xs[j, hr, zs] = jnp.where(xh == 0, high, low).astype(BF16)

        send(xs.at[j, hr], xr.at[j, hr], x_ss.at[j, hr], x_rs.at[j, hr], place(z, xl, c, oh, y))

    def reduce_x(j, hr):
        h = xl if hr == 0 else ox
        arrived(xr.at[j, hr], x_ss.at[j, hr], x_rs.at[j, hr])
        total = ysum[j, hr] + xr[j, hr].astype(F32)
        a1g[j, h, y] = total.astype(BF16).reshape(4 * rx, 512)
        for k in (1, 3, 2):
            send(a1g.at[j, h, y], a1g.at[j, h, y], a1_ss.at[j, hr, k], a1_rs.at[j, hr, y],
                 place(z, xl, c, xh, yk(k)))

    def multiply_store(j):
        for hr in range(2):
            h = xl if hr == 0 else ox
            for k in range(1, 4):
                arrived(a1g.at[j, h, yk(k)], a1_ss.at[j, hr, k], a1_rs.at[j, hr, yk(k)])

        @pl.loop(0, 4)
        def _(zt):
            total = jnp.zeros((16 * rx, 256), F32)
            for q in range(4):
                lhs = a1g[j, q // 2, :, :, (q % 2) * 256:(q % 2 + 1) * 256].reshape(16 * rx, 256)
                rhs = s_g[q, zt // 2, pl.ds(pl.multiple_of((zt % 2) * 256, 256), 256), :]
                total = total + dot_nt(lhs, rhs)
            p2[j, zt] = total.astype(BF16).reshape(4, 4 * rx, 256)

        for k in range(4):
            for l in range(4):
                if k or l:
                    send(p2.at[j, zk(k), yk(l)], r2.at[j, z, y], r2_ss.at[j, k, l], r2_rs.at[j, z, y],
                         place(zk(k), xl, c, xh, yk(l)))
        r2[j, z, y] = p2[j, z, y]

    def reduce_z(j):
        for k in range(4):
            for l in range(4):
                if k or l:
                    arrived(r2.at[j, zk(k), yk(l)], r2_ss.at[j, k, l], r2_rs.at[j, zk(k), yk(l)])
        for ys in range(4):
            total = r2[j, 0, ys].astype(F32)
            for zs in range(1, 4):
                total = total + r2[j, zs, ys].astype(F32)
            a2g[j, xl, z, :, ys * 256:(ys + 1) * 256] = total.astype(BF16)
        for k in range(4):
            for l in range(2):
                if k or l:
                    send(a2g.at[j, xl, z], a2g.at[j, xl, z], a2_ss.at[j, l, k], a2_rs.at[j, xl, z],
                         place(zk(k), ox if l else xl, c, xh, y))

    def multiply_out(j):
        for k in range(4):
            for l in range(2):
                if k or l:
                    xs_ = ox if l else xl
                    arrived(a2g.at[j, xs_, zk(k)], a2_ss.at[j, l, k], a2_rs.at[j, xs_, zk(k)])

        @pl.loop(0, 4)
        def _(t):
            total = jnp.zeros((8 * rx, 256), F32)
            part = pl.ds(pl.multiple_of((t % 2) * 256, 256), 256)
            for zs in range(4):
                lhs = a2g[j, :, zs].reshape(8 * rx, 1024)
                total = total + dot_nt(lhs, eo[t // 2, part, zs * 1024:(zs + 1) * 1024])
            ob[j, :, :, :, pl.ds(pl.multiple_of(t * 256, 256), 256)] = total.astype(BF16).reshape(2, 4, rx, 256)

        for xt in range(2):
            for zt in range(4):
                dst = out_ref.at[pl.ds(pl.multiple_of(j * rows + y * ry + xh * rx, rx), rx)]
                src = ob.at[j, xt, zt]
                here = jnp.logical_and(self_out, jnp.logical_and(xl == xt, z == zt))

                @pl.when(here)
                def _():
                    pltpu.make_async_copy(src, dst, out_rs.at[j, m]).start()

                @pl.when(jnp.logical_not(here))
                def _():
                    remote(src, dst, out_ss.at[j, xt, zt], out_rs.at[j, m],
                           place(zt, xt, c, p // 4, p % 4)).start()

    def finish(j):
        for ms in range(8):
            dst = out_ref.at[pl.ds(j * rows + (ms % 4) * ry + (ms // 4) * rx, rx)]
            arrived(dst, out_ss.at[j, 0, 0], out_rs.at[j, ms])
        for xt in range(2):
            for zt in range(4):
                here = jnp.logical_and(self_out, jnp.logical_and(xl == xt, z == zt))

                @pl.when(jnp.logical_not(here))
                def _():
                    src = ob.at[j, xt, zt]
                    remote(src, src, out_ss.at[j, xt, zt], out_rs.at[j, m],
                           place(z, xl, oc, xh, y)).wait_send()

    for j in range(NCH):
        for hr in range(2):
            reduce_y(j, hr)
            reduce_x(j, hr)
        if j == 0:
            for xls in range(2):
                for xhs in range(2):
                    qs = xls * 2 + oc
                    arrived(s_g.at[qs, xhs], s_ss.at[0], s_rs.at[qs, xhs])
    for j in range(NCH):
        multiply_store(j)
    for j in range(NCH):
        reduce_z(j)
    arrived(eo.at[oc], eo_ss, eo_rs)
    for j in range(NCH):
        multiply_out(j)
    for j in range(NCH):
        finish(j)
    for copy in sent:
        copy.wait_send()


def shards(old_store, block_map, expand_in, expand_out, attn, residual):
    tokens, width = attn.shape
    rows = tokens // NCH
    ry, rx = rows // 4, rows // 8
    dma = pltpu.SemaphoreType.DMA
    hbm = pl.BlockSpec(memory_space=pl.ANY)
    products = pl.pallas_call(
        chain_kernel,
        out_shape=jax.ShapeDtypeStruct((tokens, width), BF16),
        in_specs=[pl.BlockSpec(memory_space=pltpu.SMEM), hbm, hbm, hbm, hbm],
        out_specs=hbm,
        scratch_shapes=[
            pltpu.VMEM((4, tokens, width), BF16),
            pltpu.VMEM((4, width, 256), BF16),
            pltpu.VMEM((4, 2, 512, 256), BF16),
            pltpu.VMEM((32, 512, BLOCK), BF16),
            pltpu.VMEM((2, 512, 4096), BF16),
            pltpu.VMEM((NCH, 4, 4, ry, 1024), BF16),
            pltpu.VMEM((NCH, 2, 3, 4, ry, 512), BF16),
            pltpu.VMEM((NCH, 2, 4, rx, 512), F32),
            pltpu.VMEM((NCH, 2, 4, rx, 512), BF16),
            pltpu.VMEM((NCH, 2, 4, rx, 512), BF16),
            pltpu.VMEM((NCH, 2, 4, 4 * rx, 512), BF16),
            pltpu.VMEM((NCH, 4, 4, 4 * rx, 256), BF16),
            pltpu.VMEM((NCH, 4, 4, 4 * rx, 256), BF16),
            pltpu.VMEM((NCH, 2, 4, 4 * rx, 1024), BF16),
            pltpu.VMEM((NCH, 2, 4, rx, 1024), BF16),
            dma((4,)), dma((3,)), dma((4,)), dma((7,)), dma((4, 2)),
            dma((NCH, 4)), dma((NCH, 4)), dma, dma,
            dma((NCH, 2, 4)), dma((NCH, 2, 3)), dma((NCH, 2)), dma((NCH, 2)),
            dma((NCH, 2, 4)), dma((NCH, 2, 4)), dma((NCH, 4, 4)), dma((NCH, 4, 4)),
            dma((NCH, 2, 4)), dma((NCH, 2, 4)), dma((NCH, 2, 4)), dma((NCH, 8)),
        ],
        compiler_params=pltpu.CompilerParams(
            collective_id=0, has_side_effects=True, vmem_limit_bytes=56 * 2**20
        ),
        name="chain",
    )(block_map, old_store, expand_in, expand_out, attn)
    return (products.astype(F32) + residual.astype(F32)).astype(BF16)


def solution(mesh):
    placed = (P("mp", "dp"), P(), P("mp", "dp"), P("dp", None), P("dp", "mp"), P("dp", "mp"))
    return jax.shard_map(
        shards, mesh=mesh, in_specs=placed, out_specs=P("dp", "mp"), check_vma=False
    )
```

time: 490 us -> 129 us (0.26)
  waiting for transfers between devices: 425 us -> 0 us
  Pallas kernels: 0 us -> 127 us
  matrix products: 29.8 us -> 0 us
  between operations: 13.2 us -> 0.02 us
  local copies, waits for them, and re-layouts: 9.7 us -> 0.01 us
  other arithmetic: 9.54 us -> 2.03 us
    psum x1 -> x0, waiting for transfers between devices: 191 us -> none  [shards(): right = lax.psum(ordered.astype(jnp.bfloat16), 'dp')]
    all_gather x2 -> x0, waiting for transfers between devices: 150 us -> none  [the longest x1 93.5 us: shards(): lax.all_gather(grown, 'dp', axis=0, tiled=True)]
    pallas_call x0 -> x1, Pallas kernels: none -> 127 us  [shards(): pl.pallas_call(chain_kernel, out_shape=jax.ShapeDtypeStruct((tokens, widt...]
    reduce_scatter x1 -> x0, waiting for transfers between devices: 83.9 us -> none  [shards(): lax.psum_scatter(products.astype(jnp.bfloat16), 'mp', scatter_dimension=1...]
    dot_general x3 -> x0, matrix products: 29.8 us -> none  [the longest x2 19.7 us: contract_last(): lax.dot_general(left_side, right_side, (((1,), (1,)), ((), ())), preferre...]
    gather x1 -> x0, local copies, waits for them, and re-layouts: 8.4 us -> none  [shards(): jnp.take(stored_sum.reshape(block_count, block_rows, -1), source, axis=0)]
    convert_element_type x2 -> x1, other arithmetic: 8.75 us -> 2.03 us  [shards(): return (products.astype(F32) + residual.astype(F32)).astype(BF16)]
  transfers between devices with their start and end apart: 4 -> 0, of which waited for: 4 -> 0; matrix products, arithmetic and copies ran while one was open for 0% -> 0% of each run, Pallas kernels for 0% -> 0%
where the time goes in v1:
time: 129 us
  Pallas kernels  127 us (98%)
  other arithmetic  2.03 us (2%)
    pallas_call x1, Pallas kernels, shards(): pl.pallas_call(chain_kernel, out_shape=jax.ShapeDtypeStruct((tokens, widt...  127 us

profile of v1, /device:TPU:6, one launch (start us, length us, event | category | flops | bytes accessed | tf_op | source)
XLA Modules:
  0.0 129.0 jit_solution(14683358445314374126)
XLA Ops:
  0.0 0.0 copy-start
  0.0 127.0 %chain.1 = bf16[256,1024]{1,0:T(8,128)(2,1)} custom-call(s32[32]{0:T(128)} %map_ref.1, bf16[512,256]{1,0:T(8,128)(2,1)} %store_ref.1, bf16[1024,256]{1,0:T(8,128)(2,1)} %ein_ref.1, bf16[512,4096]{1,0:T(8,128)(2,1)} %eout_ref.1, bf16[256,1024]{1,0:T(8,128)(2,1)} %attn_ref.1), custom_call_target="tpu_custom_call" | custom-call | tf_op jit(solution)/shard_map/chain/pallas_call | solution.py:297
  127.0 0.0 copy-done
  127.0 2.0 %add_convert_fusion = bf16[256,1024]{1,0:T(8,128)(2,1)} fusion(bf16[256,1024]{1,0:T(8,128)(2,1)S(1)} %copy-done, bf16[256,1024]{1,0:T(8,128)(2,1)} %chain.1), kind=kLoop, calls=%fused_computation | loop fusion | flops 1048576 | bytes 1572864 | tf_op jit(solution)/shard_map/convert_element_type | solution.py:329
Async XLA Ops:
  0.0 127.0 %copy-start = (bf16[256,1024]{1,0:T(8,128)(2,1)S(1)}, bf16[256,1024]{1,0:T(8,128)(2,1)}, u32[]{:S(2)}) copy-start(bf16[256,1024]{1,0:T(8,128)(2,1)} %param.11) | copy-start | bytes 1572868

commit v2 on v1

--- a/solution.py
+++ b/solution.py
@@ -22,15 +22,14 @@
 
 def chain_kernel(
     map_ref, store_ref, ein_ref, eout_ref, attn_ref, out_ref,
-    attn_g, ein_g, s_g, eo_raw, eo, p1, r1, ysum, xs, xr, a1g, p2, r2, a2g, ob,
+    attn_g, ein_g, s_g, eo_raw, eo, p1, r1, ysum, xs, xr, a1g, p2, r2, a2g, ob, ow,
     loc_sem, ein_ss, ein_rs, s_ss, s_rs, at_ss, at_rs, eo_ss, eo_rs, r1_ss, r1_rs, x_ss, x_rs,
-    a1_ss, a1_rs, r2_ss, r2_rs, a2_ss, a2_rs, out_ss, out_rs,
+    a1_ss, a1_rs, r2_ss, r2_rs, a2_ss, a2_rs, diag_ss, diag_rs, ow_ss, ow_rs, out_ss, out_rs,
 ):
     d = lax.axis_index("dp")
     m = lax.axis_index("mp")
     z, xl, c = d // 4, (d // 2) % 2, d % 2
     xh, y = m // 4, m % 4
-    p = z * 2 + xl
     q0 = xl * 2 + c
     ox, oc, oh = 1 - xl, 1 - c, 1 - xh
     rows = attn_ref.shape[0] // NCH
@@ -81,30 +80,64 @@
     for k in range(1, 4):
         greet(place(z, xl, c, xh, yk(k)))
         greet(place(zk(k), xl, c, xh, y))
-        greet(place(zk(k), ox, c, xh, y))
         for l in range(1, 4):
             greet(place(zk(k), xl, c, xh, yk(l)))
-    greeted = 4 + 3 * 6
-    self_out = p == m
+    greeted = 4 + 3 * 5
+    self_out = xl == y % 2
     for ms in range(8):
         @pl.when(jnp.logical_not(jnp.logical_and(self_out, m == ms)))
         def _():
-            greet(place(m // 2, m % 2, c, ms // 4, ms % 4))
+            greet(place(z, y % 2, c, ms // 4, ms % 4))
     pl.semaphore_wait(barrier, greeted + 8 - jnp.where(self_out, 1, 0))
 
     send(ein_ref, ein_g.at[q0], ein_ss.at[0], ein_rs.at[q0], place(z, xl, oc, xh, y))
     send(ein_ref, ein_g.at[q0], ein_ss.at[1], ein_rs.at[q0], place(z, ox, c, xh, y))
-    for j in range(NCH):
-        part = pl.ds(j * rows, rows)
-        for k in (1, 3, 2):
-            send(attn_ref.at[part], attn_g.at[z, part], at_ss.at[j, k], at_rs.at[j, z],
-                 place(zk(k), xl, c, xh, y))
+    def attn_part(zs, j):
+        return attn_g.at[zs, pl.ds(j * rows, rows)]
+
+    def send_attn(src, zs, j, k, slot):
+        send(src, attn_part(zs, j), at_ss.at[j, slot], at_rs.at[j, zs], place(zk(k), xl, c, xh, y))
+
+    for j, k in ((0, 1), (1, 3), (1, 1), (0, 3)):
+        send_attn(attn_ref.at[pl.ds(j * rows, rows)], z, j, k, k // 2)
     mine = s_g.at[q0, xh]
     send(store_ref, mine, s_ss.at[0], s_rs.at[q0, xh], place(z, ox, c, xh, y))
     send(store_ref, mine, s_ss.at[1], s_rs.at[q0, xh], place(z, xl, c, oh, y))
     send(store_ref, mine, s_ss.at[2], s_rs.at[q0, xh], place(z, ox, c, oh, y))
     send(store_ref, mine, s_ss.at[3], s_rs.at[q0, xh], place(z, xl, oc, xh, y))
 
+    def half_cols(h):
+        return pl.ds(pl.multiple_of(h * 512, 512), 512)
+
+    def multiply_in(j, zs, q):
+        res = jnp.dot(attn_g[zs, pl.ds(j * rows, rows), :], ein_g[q], preferred_element_type=F32)
+        res = res.astype(BF16).reshape(4, ry, 256)
+        p1[j, :, zs, :, pl.ds(pl.multiple_of(q * 256, 256), 256)] = res
+
+    def send_partials(j, zs, hr):
+        cols = half_cols(xl if hr == 0 else ox)
+        for k in (1, 3, 2):
+            remote(p1.at[j, yk(k), zs, :, cols], r1.at[j, hr, 3 - k, zs], r1_ss.at[j, hr, k],
+                   r1_rs.at[j, hr, 3 - k], place(z, xl, c, xh, yk(k))).start()
+
+    def unit(j, zs, hr):
+        h = xl if hr == 0 else ox
+        multiply_in(j, zs, h * 2 + c)
+        multiply_in(j, zs, h * 2 + oc)
+        send_partials(j, zs, hr)
+
+    def attn_arrived(j, k):
+        arrived(attn_part(zk(k), j), at_ss.at[j, 0], at_rs.at[j, zk(k)])
+
+    local[0].wait()
+    local[1].wait()
+    for j in range(NCH):
+        multiply_in(j, z, q0)
+    arrived(ein_g.at[xl * 2 + oc], ein_ss.at[0], ein_rs.at[xl * 2 + oc])
+    for j in range(NCH):
+        multiply_in(j, z, xl * 2 + oc)
+        send_partials(j, z, 0)
+
     pltpu.make_async_copy(eo_raw, eo_raw, loc_sem.at[3]).wait()
 
     @pl.loop(0, 32)
@@ -115,41 +148,27 @@
 
     send(eo.at[c], eo.at[c], eo_ss, eo_rs, place(z, xl, oc, xh, y))
 
-    local[0].wait()
-    local[1].wait()
-
-    def multiply_in(j, q):
-        lhs = attn_g[:, pl.ds(j * rows, rows), :].reshape(4 * rows, -1)
-        res = jnp.dot(lhs, ein_g[q], preferred_element_type=F32).astype(BF16)
-        res = res.reshape(4, 4, ry, 256)
-        cols = pl.ds(pl.multiple_of(q * 256, 256), 256)
-        for yt in range(4):
-            p1[j, yt, :, :, cols] = res[:, yt]
-
-    def half_cols(h):
-        return pl.ds(pl.multiple_of(h * 512, 512), 512)
-
-    def send_partials(j, hr):
-        h = xl if hr == 0 else ox
-        for k in (1, 3, 2):
-            send(p1.at[j, yk(k), :, :, half_cols(h)], r1.at[j, hr, 3 - k], r1_ss.at[j, hr, k],
-                 r1_rs.at[j, hr, 3 - k], place(z, xl, c, xh, yk(k)))
-
-    for j in range(NCH):
-        for k in (1, 3, 2):
-            arrived(attn_g.at[zk(k), pl.ds(j * rows, rows)], at_ss.at[j, k], at_rs.at[j, zk(k)])
-        for hr in range(2):
-            qa = (xl if hr == 0 else ox) * 2 + c
-            qb = (xl if hr == 0 else ox) * 2 + oc
-            if j == 0:
-                if hr == 1:
-                    arrived(ein_g.at[qa], ein_ss.at[1], ein_rs.at[qa])
-                    send(ein_g.at[qa], ein_g.at[qa], ein_ss.at[2], ein_rs.at[qa], place(z, xl, oc, xh, y))
-            multiply_in(j, qa)
-            if j == 0:
-                arrived(ein_g.at[qb], ein_ss.at[0], ein_rs.at[qb])
-            multiply_in(j, qb)
-            send_partials(j, hr)
+    attn_arrived(0, 3)
+    send_attn(attn_part(zk(3), 0), zk(3), 0, 1, 2)
+    attn_arrived(1, 1)
+    send_attn(attn_part(zk(1), 1), zk(1), 1, 3, 2)
+    unit(0, zk(3), 0)
+    unit(1, zk(1), 0)
+    qa = ox * 2 + c
+    arrived(ein_g.at[qa], ein_ss.at[1], ein_rs.at[qa])
+    send(ein_g.at[qa], ein_g.at[qa], ein_ss.at[2], ein_rs.at[qa], place(z, xl, oc, xh, y))
+    attn_arrived(1, 3)
+    unit(1, zk(3), 0)
+    attn_arrived(0, 1)
+    unit(0, zk(1), 0)
+    arrived(ein_g.at[ox * 2 + oc], ein_ss.at[2], ein_rs.at[ox * 2 + oc])
+    for j in range(NCH):
+        for k in (0, 1, 3):
+            unit(j, zk(k), 1)
+    for j in range(NCH):
+        attn_arrived(j, 2)
+        unit(j, zk(2), 0)
+        unit(j, zk(2), 1)
 
     local[2].wait()
     for i, (xls, xhs) in enumerate(((ox, xh), (xl, oh), (ox, oh))):
@@ -215,18 +234,27 @@
             for zs in range(1, 4):
                 total = total + r2[j, zs, ys].astype(F32)
             a2g[j, xl, z, :, ys * 256:(ys + 1) * 256] = total.astype(BF16)
-        for k in range(4):
-            for l in range(2):
-                if k or l:
-                    send(a2g.at[j, xl, z], a2g.at[j, xl, z], a2_ss.at[j, l, k], a2_rs.at[j, xl, z],
-                         place(zk(k), ox if l else xl, c, xh, y))
+        mine = a2g.at[j, xl, z]
+        send(mine, mine, a2_ss.at[j, 0], a2_rs.at[j, xl, z], place(z, ox, c, xh, y))
+        for k in (1, 3, 2):
+            send(mine, mine, a2_ss.at[j, k], a2_rs.at[j, xl, z], place(zk(k), xl, c, xh, y))
+
+    def relay(j):
+        near, far = pl.ds(0, 2 * rx), pl.ds(2 * rx, 2 * rx)
+        arrived(a2g.at[j, ox, z], a2_ss.at[j, 0], a2_rs.at[j, ox, z])
+        for k in (1, 3, 2):
+            half = a2g.at[j, ox, z, near]
+            send(half, half, diag_ss.at[j, 0, k], diag_rs.at[j, 0, z], place(zk(k), xl, c, xh, y))
+        for k in (1, 3, 2):
+            arrived(a2g.at[j, xl, zk(k)], a2_ss.at[j, k], a2_rs.at[j, xl, zk(k)])
+            half = a2g.at[j, xl, zk(k), far]
+            send(half, half, diag_ss.at[j, 1, k], diag_rs.at[j, 1, zk(k)], place(z, ox, c, xh, y))
 
     def multiply_out(j):
-        for k in range(4):
-            for l in range(2):
-                if k or l:
-                    xs_ = ox if l else xl
-                    arrived(a2g.at[j, xs_, zk(k)], a2_ss.at[j, l, k], a2_rs.at[j, xs_, zk(k)])
+        near, far = pl.ds(0, 2 * rx), pl.ds(2 * rx, 2 * rx)
+        for k in range(1, 4):
+            arrived(a2g.at[j, ox, zk(k), near], diag_ss.at[j, 0, k], diag_rs.at[j, 0, zk(k)])
+            arrived(a2g.at[j, ox, zk(k), far], diag_ss.at[j, 1, k], diag_rs.at[j, 1, zk(k)])
 
         @pl.loop(0, 4)
         def _(t):
@@ -235,36 +263,53 @@
             for zs in range(4):
                 lhs = a2g[j, :, zs].reshape(8 * rx, 1024)
                 total = total + dot_nt(lhs, eo[t // 2, part, zs * 1024:(zs + 1) * 1024])
-            ob[j, :, :, :, pl.ds(pl.multiple_of(t * 256, 256), 256)] = total.astype(BF16).reshape(2, 4, rx, 256)
-
-        for xt in range(2):
-            for zt in range(4):
-                dst = out_ref.at[pl.ds(pl.multiple_of(j * rows + y * ry + xh * rx, rx), rx)]
-                src = ob.at[j, xt, zt]
-                here = jnp.logical_and(self_out, jnp.logical_and(xl == xt, z == zt))
+            res = total.astype(BF16).reshape(2, 4, rx, 256)
+            for xt in range(2):
+                ob[j, :, xt, :, pl.ds(pl.multiple_of(t * 256, 256), 256)] = res[xt]
+
+        for k in (2, 1, 3):
+            send(ob.at[j, zk(k)], ow.at[j, z], ow_ss.at[j, k], ow_rs.at[j, z], place(zk(k), xl, c, xh, y))
+
+    def out_copy(j, k, xt):
+        zs = zk(k)
+        src = ob.at[j, z, xt] if k == 0 else ow.at[j, zs, xt]
+        dst = out_ref.at[pl.ds(pl.multiple_of(j * rows + y * ry + xh * rx, rx), rx)]
+        here = jnp.logical_and(xl == xt, jnp.logical_and(zs // 2 == xh, (zs % 2) * 2 + xl == y))
+        copy = remote(src, dst, out_ss.at[j, xt, k], out_rs.at[j, m], place(z, xt, c, zs // 2, (zs % 2) * 2 + xl))
+        return here, copy, lambda: pltpu.make_async_copy(src, dst, out_rs.at[j, m]).start()
+
+    def relay_out(j):
+        for k in (0, 1, 3, 2):
+            if k:
+                arrived(ow.at[j, zk(k)], ow_ss.at[j, k], ow_rs.at[j, zk(k)])
+            for xt in range(2):
+                here, copy, own = out_copy(j, k, xt)
 
                 @pl.when(here)
                 def _():
-                    pltpu.make_async_copy(src, dst, out_rs.at[j, m]).start()
+                    own()
 
                 @pl.when(jnp.logical_not(here))
                 def _():
-                    remote(src, dst, out_ss.at[j, xt, zt], out_rs.at[j, m],
-                           place(zt, xt, c, p // 4, p % 4)).start()
+                    copy.start()
 
     def finish(j):
         for ms in range(8):
             dst = out_ref.at[pl.ds(j * rows + (ms % 4) * ry + (ms // 4) * rx, rx)]
             arrived(dst, out_ss.at[j, 0, 0], out_rs.at[j, ms])
-        for xt in range(2):
-            for zt in range(4):
-                here = jnp.logical_and(self_out, jnp.logical_and(xl == xt, z == zt))
+        for k in range(4):
+            for xt in range(2):
+                here, copy, own = out_copy(j, k, xt)
 
                 @pl.when(jnp.logical_not(here))
                 def _():
-                    src = ob.at[j, xt, zt]
-                    remote(src, src, out_ss.at[j, xt, zt], out_rs.at[j, m],
-                           place(z, xl, oc, xh, y)).wait_send()
+                    copy.wait_send()
+        for hr in range(2):
+            cols = half_cols(xl if hr == 0 else ox)
+            for k in range(1, 4):
+                src = p1.at[j, yk(k), :, :, cols]
+                remote(src, r1.at[j, hr, 3 - k], r1_ss.at[j, hr, k], r1_rs.at[j, hr, 3 - k],
+                       place(z, xl, c, xh, yk(k))).wait_send()
 
     for j in range(NCH):
         for hr in range(2):
@@ -281,7 +326,11 @@
         reduce_z(j)
     arrived(eo.at[oc], eo_ss, eo_rs)
     for j in range(NCH):
+        relay(j)
+    for j in range(NCH):
         multiply_out(j)
+    for j in range(NCH):
+        relay_out(j)
     for j in range(NCH):
         finish(j)
     for copy in sent:
@@ -314,12 +363,14 @@
             pltpu.VMEM((NCH, 4, 4, 4 * rx, 256), BF16),
             pltpu.VMEM((NCH, 4, 4, 4 * rx, 256), BF16),
             pltpu.VMEM((NCH, 2, 4, 4 * rx, 1024), BF16),
-            pltpu.VMEM((NCH, 2, 4, rx, 1024), BF16),
+            pltpu.VMEM((NCH, 4, 2, rx, 1024), BF16),
+            pltpu.VMEM((NCH, 4, 2, rx, 1024), BF16),
             dma((4,)), dma((3,)), dma((4,)), dma((7,)), dma((4, 2)),
-            dma((NCH, 4)), dma((NCH, 4)), dma, dma,
+            dma((NCH, 3)), dma((NCH, 4)), dma, dma,
             dma((NCH, 2, 4)), dma((NCH, 2, 3)), dma((NCH, 2)), dma((NCH, 2)),
             dma((NCH, 2, 4)), dma((NCH, 2, 4)), dma((NCH, 4, 4)), dma((NCH, 4, 4)),
-            dma((NCH, 2, 4)), dma((NCH, 2, 4)), dma((NCH, 2, 4)), dma((NCH, 8)),
+            dma((NCH, 4)), dma((NCH, 2, 4)), dma((NCH, 2, 4)), dma((NCH, 2, 4)),
+            dma((NCH, 4)), dma((NCH, 4)), dma((NCH, 2, 4)), dma((NCH, 8)),
         ],
         compiler_params=pltpu.CompilerParams(
             collective_id=0, has_side_effects=True, vmem_limit_bytes=56 * 2**20

time: 129 us -> 106 us (0.82)
  Pallas kernels: 127 us -> 104 us
    pallas_call x1, Pallas kernels: 127 us -> 104 us  [shards(): pl.pallas_call(chain_kernel, out_shape=jax.ShapeDtypeStruct((tokens, widt...]
where the time goes in v2:
time: 106 us
  Pallas kernels  104 us (98%)
  other arithmetic  2.03 us (2%)
    pallas_call x1, Pallas kernels, shards(): pl.pallas_call(chain_kernel, out_shape=jax.ShapeDtypeStruct((tokens, widt...  104 us

profile of v2, /device:TPU:6, one launch (start us, length us, event | category | flops | bytes accessed | tf_op | source)
XLA Modules:
  0.0 106.1 jit_solution(2802466645022539904)
XLA Ops:
  0.0 0.0 copy-start
  0.0 104.0 %chain.1 = bf16[256,1024]{1,0:T(8,128)(2,1)} custom-call(s32[32]{0:T(128)} %map_ref.1, bf16[512,256]{1,0:T(8,128)(2,1)} %store_ref.1, bf16[1024,256]{1,0:T(8,128)(2,1)} %ein_ref.1, bf16[512,4096]{1,0:T(8,128)(2,1)} %eout_ref.1, bf16[256,1024]{1,0:T(8,128)(2,1)} %attn_ref.1), custom_call_target="tpu_custom_call" | custom-call | tf_op jit(solution)/shard_map/chain/pallas_call | solution.py:346
  104.0 0.0 copy-done
  104.0 2.0 %add_convert_fusion = bf16[256,1024]{1,0:T(8,128)(2,1)} fusion(bf16[256,1024]{1,0:T(8,128)(2,1)S(1)} %copy-done, bf16[256,1024]{1,0:T(8,128)(2,1)} %chain.1), kind=kLoop, calls=%fused_computation | loop fusion | flops 1048576 | bytes 1572864 | tf_op jit(solution)/shard_map/convert_element_type | solution.py:380
Async XLA Ops:
  0.0 104.0 %copy-start = (bf16[256,1024]{1,0:T(8,128)(2,1)S(1)}, bf16[256,1024]{1,0:T(8,128)(2,1)}, u32[]{:S(2)}) copy-start(bf16[256,1024]{1,0:T(8,128)(2,1)} %param.11) | copy-start | bytes 1572868

commit v3 on v1

v3 whole, which is shorter than its diff:
```python
import jax
import jax.numpy as jnp
from jax import lax
from jax.experimental import pallas as pl
from jax.experimental.pallas import tpu as pltpu
from jax.sharding import PartitionSpec as P

MESH = pl.DeviceIdType.MESH
BLOCK = 128
NCH = 2
NEAR = 32
F32 = jnp.float32
BF16 = jnp.bfloat16


def place(z, xl, c, xh, y):
    return {"dp": z * 4 + xl * 2 + c, "mp": xh * 4 + y}


def dot_nt(a, b):
    return lax.dot_general(a, b, (((1,), (1,)), ((), ())), preferred_element_type=F32)


def chain_kernel(
    map_ref, store_ref, ein_ref, eout_ref, attn_ref, out_ref,
    attn_g, ein_g, s_g, eo_raw, eo, p1, r1, ysum, xs, xr, a1g, p2, r2, rm, q2, a2g, ob, ow,
    loc_sem, ein_ss, ein_rs, s_ss, s_rs, at_ss, at_rs, eo_ss, eo_rs, r1_ss, r1_rs, x_ss, x_rs,
    a1_ss, a1_rs, r2_ss, r2_rs, rm_ss, rm_rs, q2_ss, q2_rs, a2_ss, a2_rs, diag_ss, diag_rs, ow_ss, ow_rs, out_ss, out_rs,
):
    d = lax.axis_index("dp")
    m = lax.axis_index("mp")
    z, xl, c = d // 4, (d // 2) % 2, d % 2
    xh, y = m // 4, m % 4
    q0 = xl * 2 + c
    ox, oc, oh = 1 - xl, 1 - c, 1 - xh
    rows = attn_ref.shape[0] // NCH
    ry, rx = rows // 4, rows // 8
    sent = []

    def remote(src, dst, ss, rs, target):
        return pltpu.make_async_remote_copy(
            src_ref=src, dst_ref=dst, send_sem=ss, recv_sem=rs, device_id=target, device_id_type=MESH
        )

    def send(src, dst, ss, rs, target):
        copy = remote(src, dst, ss, rs, target)
        copy.start()
        sent.append(copy)

    def arrived(dst, ss, rs):
        remote(dst, dst, ss, rs, place(z, xl, oc, xh, y)).wait_recv()

    def zk(k):
        return lax.rem(z + k, 4)

    def yk(k):
        return lax.rem(y + k, 4)

    local = [
        pltpu.make_async_copy(attn_ref, attn_g.at[z], loc_sem.at[0]),
        pltpu.make_async_copy(ein_ref.at[:, :128], ein_g.at[q0, 0], loc_sem.at[1]),
        pltpu.make_async_copy(ein_ref.at[:, 128:], ein_g.at[q0, 1], loc_sem.at[4]),
        pltpu.make_async_copy(store_ref, s_g.at[q0, xh], loc_sem.at[2]),
    ]
    for copy in local:
        copy.start()

    @pl.loop(0, 32)
    def _(t):
        cols = pl.ds(pl.multiple_of(t * BLOCK, BLOCK), BLOCK)
        pltpu.make_async_copy(eout_ref.at[:, cols], eo_raw.at[t], loc_sem.at[3]).start()

    barrier = pltpu.get_barrier_semaphore()

    def greet(target):
        pl.semaphore_signal(barrier, inc=1, device_id=target, device_id_type=MESH)

    greet(place(z, xl, oc, xh, y))
    greet(place(z, ox, c, xh, y))
    greet(place(z, xl, c, oh, y))
    greet(place(z, ox, c, oh, y))
    for k in range(1, 4):
        greet(place(z, xl, c, xh, yk(k)))
        greet(place(zk(k), xl, c, xh, y))
    pl.semaphore_wait(barrier, 10)

    for a in range(2):
        src = ein_ref.at[:, a * 128:(a + 1) * 128]
        send(src, ein_g.at[q0, a], ein_ss.at[a, 0], ein_rs.at[q0, a], place(z, xl, oc, xh, y))
        send(src, ein_g.at[q0, a], ein_ss.at[a, 1], ein_rs.at[q0, a], place(z, ox, c, xh, y))

    def attn_part(zs, j):
        return attn_g.at[zs, pl.ds(j * rows, rows)]

    def send_attn(j):
        for k in (1, 3):
            send(attn_ref.at[pl.ds(j * rows, rows)], attn_part(z, j), at_ss.at[j, k], at_rs.at[j, z],
                 place(zk(k), xl, c, xh, y))

    def attn_arrived(j, k):
        arrived(attn_part(zk(k), j), at_ss.at[j, k], at_rs.at[j, zk(k)])

    def attn_near(j):
        half = rows // 2
        for k in (1, 3):
            attn_arrived(j, 4 - k)
            src = attn_g.at[zk(4 - k), pl.ds(j * rows + (k // 2) * half, half)]
            send(src, src, at_ss.at[j, k - 1], at_rs.at[j, zk(4 - k)], place(zk(k), xl, c, xh, y))

    send_attn(0)

    mine = s_g.at[q0, xh]
    send(store_ref, mine, s_ss.at[0], s_rs.at[q0, xh], place(z, ox, c, oh, y))
    send(store_ref, mine, s_ss.at[1], s_rs.at[q0, xh], place(z, xl, oc, xh, y))

    def half_cols(h):
        return pl.ds(pl.multiple_of(h * 512, 512), 512)

    def multiply_in(j, zs, hr, a):
        h = xl if hr == 0 else ox
        rhs = jnp.concatenate([ein_g[h * 2, a], ein_g[h * 2 + 1, a]], axis=1)
        res = jnp.dot(attn_g[zs, pl.ds(j * rows, rows), :], rhs, preferred_element_type=F32)
        res = res.astype(BF16).reshape(4, ry, 256)
        p1[j, :, zs, :, pl.ds(pl.multiple_of(h * 512 + a * 256, 256), 256)] = res

    def send_partials(j, zs, hr, first=0, width=512):
        cols = pl.ds(pl.multiple_of((xl if hr == 0 else ox) * 512 + first, 256), width)
        for k in (1, 3, 2):
            remote(p1.at[j, yk(k), zs, :, cols], r1.at[j, hr, 3 - k, zs, :, first:first + width],
                   r1_ss.at[j, hr, k], r1_rs.at[j, hr, 3 - k], place(z, xl, c, xh, yk(k))).start()

    def unit(j, zs, hr, a=None):
        if a is None:
            multiply_in(j, zs, hr, 0)
            multiply_in(j, zs, hr, 1)
            send_partials(j, zs, hr)
        else:
            multiply_in(j, zs, hr, a)
            send_partials(j, zs, hr, a * 256, 256)

    def compute(j, zs, hr):
        multiply_in(j, zs, hr, 0)
        multiply_in(j, zs, hr, 1)

    def ein_far(a):
        qa = ox * 2 + c
        arrived(ein_g.at[qa, a], ein_ss.at[a, 1], ein_rs.at[qa, a])
        send(ein_g.at[qa, a], ein_g.at[qa, a], ein_ss.at[a, 2], ein_rs.at[qa, a], place(z, xl, oc, xh, y))

    def ein_far_core(a):
        qb = ox * 2 + oc
        arrived(ein_g.at[qb, a], ein_ss.at[a, 2], ein_rs.at[qb, a])

    def send_store():
        send(store_ref, mine, s_ss.at[2], s_rs.at[q0, xh], place(z, ox, c, xh, y))

    def relay_store(i, xls, xhs):
        block = s_g.at[xls * 2 + c, xhs]
        arrived(block, s_ss.at[0], s_rs.at[xls * 2 + c, xhs])
        send(block, block, s_ss.at[3 + i], s_rs.at[xls * 2 + c, xhs], place(z, xl, oc, xh, y))
        if i == 1:
            send(block, block, s_ss.at[6], s_rs.at[xls * 2 + c, xhs], place(z, ox, c, oh, y))

    local[0].wait()
    local[1].wait()
    local[2].wait()
    for a in range(2):
        arrived(ein_g.at[xl * 2 + oc, a], ein_ss.at[a, 0], ein_rs.at[xl * 2 + oc, a])
    unit(0, z, 0)
    unit(1, z, 0)

    pltpu.make_async_copy(eo_raw, eo_raw, loc_sem.at[3]).wait()

    @pl.loop(0, 32)
    def _(t):
        zs, ys, b = t // 8, (t // 2) % 4, t % 2
        s = ((zs // 2) * 4 + ys) * 4 + (zs % 2) * 2 + b
        eo[c, pl.ds(pl.multiple_of(t * BLOCK, BLOCK), BLOCK), :] = eo_raw[map_ref[s]].T

    send(eo.at[c], eo.at[c], eo_ss, eo_rs, place(z, xl, oc, xh, y))

    attn_near(0)
    send_attn(1)
    unit(0, zk(1), 0)
    unit(0, zk(3), 0)
    ein_far(0)
    ein_far_core(0)
    for k in (0, 1, 3):
        unit(0, zk(k), 1, 0)
    attn_arrived(0, 2)
    unit(0, zk(2), 0)
    unit(0, zk(2), 1, 0)
    ein_far(1)
    send_store()
    ein_far_core(1)
    for k in range(4):
        unit(0, zk(k), 1, 1)
    unit(1, z, 1)
    relay_store(0, ox, oh)
    attn_near(1)

    def store_arrived():
        local[3].wait()
        for xls in range(2):
            for xhs in range(2):
                qs = xls * 2 + oc
                arrived(s_g.at[qs, xhs], s_ss.at[0], s_rs.at[qs, xhs])

    def reduce_y(j, hr):
        h = xl if hr == 0 else ox
        cols = half_cols(h)
        for k in range(3):
            arrived(r1.at[j, hr, k], r1_ss.at[j, hr, 1], r1_rs.at[j, hr, k])

        @pl.loop(0, 4)
        def _(zs):
            total = p1[j, y, zs, :, cols].astype(F32)
            for k in range(3):
                total = total + r1[j, hr, k, zs].astype(F32)
            low, high = total[:rx], total[rx:]
            ysum[j, hr, zs] = jnp.where(xh == 0, low, high)
            xs[j, hr, zs] = jnp.where(xh == 0, high, low).astype(BF16)

        send(xs.at[j, hr], xr.at[j, hr], x_ss.at[j, hr], x_rs.at[j, hr], place(z, xl, c, oh, y))

    def reduce_x(j, hr):
        h = xl if hr == 0 else ox
        arrived(xr.at[j, hr], x_ss.at[j, hr], x_rs.at[j, hr])
        total = ysum[j, hr] + xr[j, hr].astype(F32)
        a1g[j, h, y] = total.astype(BF16).reshape(4 * rx, 512)
        for k in (1, 3, 2):
            send(a1g.at[j, h, y], a1g.at[j, h, y], a1_ss.at[j, hr, k], a1_rs.at[j, hr, y],
                 place(z, xl, c, xh, yk(k)))

    def multiply_store(j):
        for hr in range(2):
            h = xl if hr == 0 else ox
            for k in range(1, 4):
                arrived(a1g.at[j, h, yk(k)], a1_ss.at[j, hr, k], a1_rs.at[j, hr, yk(k)])

        for k in (2, 1, 3, 0):
            zt = zk(k)
            total = jnp.zeros((16 * rx, 256), F32)
            for q in range(4):
                first = (q % 2) * 128
                lhs = jnp.concatenate(
                    [a1g[j, q // 2, :, :, first:first + 128], a1g[j, q // 2, :, :, first + 256:first + 384]], axis=2
                ).reshape(16 * rx, 256)
                rhs = s_g[q, zt // 2, pl.ds(pl.multiple_of((zt % 2) * 256, 256), 256), :]
                total = total + dot_nt(lhs, rhs)
            p2[j, zt] = total.astype(BF16).reshape(4, 4 * rx, 256)
            if j == 0:
                if k:
                    send(p2.at[j, zt], r2.at[3 - k], r2_ss.at[k], r2_rs.at[3 - k], place(zt, xl, c, xh, y))
            else:
                for l in (2, 1, 3, 0):
                    if k or l:
                        send(p2.at[j, zt, yk(l)], rm.at[z, y], rm_ss.at[k, l], rm_rs.at[z, y],
                             place(zt, xl, c, xh, yk(l)))

    def a2_cols(ys):
        return pl.ds(pl.multiple_of(ys * 256, 256), 256)

    def reduce_z():
        for k in range(1, 4):
            arrived(r2.at[3 - k], r2_ss.at[k], r2_rs.at[3 - k])

        @pl.loop(0, 4)
        def _(yt):
            total = p2[0, z, yt].astype(F32)
            for k in range(3):
                total = total + r2[k, yt].astype(F32)
            q2[yt] = total.astype(BF16)

        for k in (2, 1, 3):
            send(q2.at[yk(k)], a2g.at[0, xl, z, :, a2_cols(y)], q2_ss.at[k], q2_rs.at[y], place(z, xl, c, xh, yk(k)))
        a2g[0, xl, z, :, a2_cols(y)] = q2[y]

    def reduce_zy():
        rm[z, y] = p2[1, z, y]
        for k in range(4):
            for l in range(4):
                if k or l:
                    arrived(rm.at[zk(k), yk(l)], rm_ss.at[k, l], rm_rs.at[zk(k), yk(l)])

        @pl.loop(0, 4)
        def _(ys):
            total = rm[0, ys].astype(F32)
            for zs in range(1, 4):
                total = total + rm[zs, ys].astype(F32)
            a2g[1, xl, z, :, a2_cols(ys)] = total.astype(BF16)

    def spread(j):
        if j == 0:
            for k in range(1, 4):
                arrived(a2g.at[j, xl, z, :, a2_cols(yk(k))], q2_ss.at[k], q2_rs.at[yk(k)])
        for half in (0, 1):
            to_x, to_z = a2g.at[j, xl, z, parts[half]], a2g.at[j, xl, z, parts[1 - half]]
            send(to_x, to_x, a2_ss.at[j, half, 0], a2_rs.at[j, half, xl, z], place(z, ox, c, xh, y))
            for k in (1, 3, 2):
                send(to_z, to_z, a2_ss.at[j, 1 - half, k], a2_rs.at[j, 1 - half, xl, z], place(zk(k), xl, c, xh, y))

    parts = (pl.ds(0, NEAR), pl.ds(NEAR, 4 * rx - NEAR))

    def block_arrived(j, half, xs_, k):
        arrived(a2g.at[j, xs_, zk(k), parts[half]], a2_ss.at[j, half, k], a2_rs.at[j, half, xs_, zk(k)])

    def relay_x(j):
        block_arrived(j, 0, ox, 0)
        for k in (1, 3, 2):
            half = a2g.at[j, ox, z, parts[0]]
            send(half, half, diag_ss.at[j, 0, k], diag_rs.at[j, 0, z], place(zk(k), xl, c, xh, y))

    def relay_z(j):
        for k in (1, 3, 2):
            block_arrived(j, 1, xl, k)
            half = a2g.at[j, xl, zk(k), parts[1]]
            send(half, half, diag_ss.at[j, 1, k], diag_rs.at[j, 1, zk(k)], place(z, ox, c, xh, y))

    def multiply_out(j):
        block_arrived(j, 1, ox, 0)
        for k in range(1, 4):
            block_arrived(j, 0, xl, k)
            for half in range(2):
                arrived(a2g.at[j, ox, zk(k), parts[half]], diag_ss.at[j, half, k], diag_rs.at[j, half, zk(k)])
        for half in range(2):
            @pl.loop(0, 2)
            def _(t):
                total = jnp.zeros((8 * rx, 256), F32)
                part = pl.ds(pl.multiple_of(t * 256, 256), 256)
                for zs in range(4):
                    lhs = a2g[j, :, zs].reshape(8 * rx, 1024)
                    rhs = eo[half, zs * 1024:(zs + 1) * 1024, part]
                    total = total + jnp.dot(lhs, rhs, preferred_element_type=F32)
                res = total.astype(BF16).reshape(2, 4, rx, 256)
                for xt in range(2):
                    ob[j, half, :, xt, :, part] = res[xt]

            for k in (2, 1, 3):
                send(ob.at[j, half, zk(k)], ow.at[j, half, z], ow_ss.at[j, half, k], ow_rs.at[j, half, z],
                     place(zk(k), xl, c, xh, y))

    def out_copy(j, half, k, xt):
        zs = zk(k)
        src = ow.at[j, half, zs, xt] if k else ob.at[j, half, z, xt]
        dst = out_ref.at[pl.ds(pl.multiple_of(j * rows + y * ry + xh * rx, rx), rx), pl.ds(half * 512, 512)]
        here = jnp.logical_and(xl == xt, jnp.logical_and(zs // 2 == xh, (zs % 2) * 2 + xl == y))
        copy = remote(src, dst, out_ss.at[j, half, k, xt], out_rs.at[j, half, m],
                      place(z, xt, c, zs // 2, (zs % 2) * 2 + xl))
        return here, copy, lambda: pltpu.make_async_copy(src, dst, out_rs.at[j, half, m]).start()

    def relay_out(j, half):
        for k in (0, 1, 3, 2):
            if k:
                arrived(ow.at[j, half, zk(k)], ow_ss.at[j, half, k], ow_rs.at[j, half, zk(k)])
            for xt in range(2):
                here, copy, own = out_copy(j, half, k, xt)
                pl.when(here)(own)
                pl.when(jnp.logical_not(here))(copy.start)

    def finish(j):
        for half in range(2):
            for ms in range(8):
                dst = out_ref.at[pl.ds(j * rows + (ms % 4) * ry + (ms // 4) * rx, rx), pl.ds(half * 512, 512)]
                arrived(dst, out_ss.at[j, 0, 0, 0], out_rs.at[j, half, ms])
            for k in range(4):
                for xt in range(2):
                    here, copy, own = out_copy(j, half, k, xt)
                    pl.when(jnp.logical_not(here))(copy.wait_send)
        for hr in range(2):
            cols = half_cols(xl if hr == 0 else ox)
            for k in range(1, 4):
                remote(p1.at[j, yk(k), :, :, cols], r1.at[j, hr, 3 - k], r1_ss.at[j, hr, k], r1_rs.at[j, hr, 3 - k],
                       place(z, xl, c, xh, yk(k))).wait_send()

    reduce_y(0, 0)
    relay_store(1, ox, xh)
    compute(1, zk(1), 0)
    compute(1, zk(3), 0)
    reduce_x(0, 0)
    send_partials(1, zk(1), 0)
    compute(1, zk(1), 1)
    compute(1, zk(3), 1)
    reduce_y(0, 1)
    attn_arrived(1, 2)
    compute(1, zk(2), 0)
    compute(1, zk(2), 1)
    reduce_x(0, 1)
    for hr in range(2):
        for k in (1, 3, 2):
            if k != 1 or hr != 0:
                send_partials(1, zk(k), hr)
    relay_store(2, xl, oh)
    store_arrived()
    multiply_store(0)
    reduce_y(1, 0)
    reduce_y(1, 1)
    reduce_x(1, 0)
    reduce_z()
    reduce_x(1, 1)
    spread(0)
    relay_x(0)
    multiply_store(1)
    relay_z(0)
    reduce_zy()
    spread(1)
    arrived(eo.at[oc], eo_ss, eo_rs)
    relay_x(1)
    multiply_out(0)
    relay_z(1)
    relay_out(0, 0)
    relay_out(0, 1)
    multiply_out(1)
    relay_out(1, 0)
    relay_out(1, 1)
    for j in range(NCH):
        finish(j)
    for copy in sent:
        copy.wait_send()


def shards(old_store, block_map, expand_in, expand_out, attn, residual):
    tokens, width = attn.shape
    rows = tokens // NCH
    ry, rx = rows // 4, rows // 8
    dma = pltpu.SemaphoreType.DMA
    hbm = pl.BlockSpec(memory_space=pl.ANY)
    products = pl.pallas_call(
        chain_kernel,
        out_shape=jax.ShapeDtypeStruct((tokens, width), BF16),
        in_specs=[pl.BlockSpec(memory_space=pltpu.SMEM), hbm, hbm, hbm, hbm],
        out_specs=hbm,
        scratch_shapes=[
            pltpu.VMEM((4, tokens, width), BF16),
            pltpu.VMEM((4, 2, width, 128), BF16),
            pltpu.VMEM((4, 2, 512, 256), BF16),
            pltpu.VMEM((32, 512, BLOCK), BF16),
            pltpu.VMEM((2, 4096, 512), BF16),
            pltpu.VMEM((NCH, 4, 4, ry, 1024), BF16),
            pltpu.VMEM((NCH, 2, 3, 4, ry, 512), BF16),
            pltpu.VMEM((NCH, 2, 4, rx, 512), F32),
            pltpu.VMEM((NCH, 2, 4, rx, 512), BF16),
            pltpu.VMEM((NCH, 2, 4, rx, 512), BF16),
            pltpu.VMEM((NCH, 2, 4, 4 * rx, 512), BF16),
            pltpu.VMEM((NCH, 4, 4, 4 * rx, 256), BF16),
            pltpu.VMEM((3, 4, 4 * rx, 256), BF16),
            pltpu.VMEM((4, 4, 4 * rx, 256), BF16),
            pltpu.VMEM((4, 4 * rx, 256), BF16),
            pltpu.VMEM((NCH, 2, 4, 4 * rx, 1024), BF16),
            pltpu.VMEM((NCH, 2, 4, 2, rx, 512), BF16),
            pltpu.VMEM((NCH, 2, 4, 2, rx, 512), BF16),
            dma((5,)), dma((2, 3)), dma((4, 2)), dma((7,)), dma((4, 2)),
            dma((NCH, 4)), dma((NCH, 4)), dma, dma,
            dma((NCH, 2, 4)), dma((NCH, 2, 3)), dma((NCH, 2)), dma((NCH, 2)),
            dma((NCH, 2, 4)), dma((NCH, 2, 4)), dma((4,)), dma((3,)), dma((4, 4)), dma((4, 4)), dma((4,)), dma((4,)),
            dma((NCH, 2, 4)), dma((NCH, 2, 2, 4)), dma((NCH, 2, 4)), dma((NCH, 2, 4)),
            dma((NCH, 2, 4)), dma((NCH, 2, 4)), dma((NCH, 2, 4, 2)), dma((NCH, 2, 8)),
        ],
        compiler_params=pltpu.CompilerParams(
            collective_id=0, has_side_effects=True, vmem_limit_bytes=56 * 2**20
        ),
        name="chain",
    )(block_map, old_store, expand_in, expand_out, attn)
    return (products.astype(F32) + residual.astype(F32)).astype(BF16)


def solution(mesh):
    placed = (P("mp", "dp"), P(), P("mp", "dp"), P("dp", None), P("dp", "mp"), P("dp", "mp"))
    return jax.shard_map(
        shards, mesh=mesh, in_specs=placed, out_specs=P("dp", "mp"), check_vma=False
    )
```

time: 129 us -> 95.9 us (0.74)
  Pallas kernels: 127 us -> 93.3 us
    pallas_call x1, Pallas kernels: 127 us -> 93.3 us  [shards(): pl.pallas_call(chain_kernel, out_shape=jax.ShapeDtypeStruct((tokens, widt...]
where the time goes in v3:
time: 95.9 us; the launch traced here: 95.3 us
  Pallas kernels  93.3 us (97%)
  other arithmetic  2.03 us (2%)
    pallas_call x1, Pallas kernels, shards(): pl.pallas_call(chain_kernel, out_shape=jax.ShapeDtypeStruct((tokens, widt...  93.3 us
    convert_element_type x1, other arithmetic, shards(): return (products.astype(F32) + residual.astype(F32)).astype(BF16)  2.03 us

profile of v3, /device:TPU:6, one launch (start us, length us, event | category | flops | bytes accessed | tf_op | source)
XLA Modules:
  0.0 95.3 jit_solution(17306761803877586473)
XLA Ops:
  0.0 0.0 copy-start
  0.0 93.3 %chain.1 = bf16[256,1024]{1,0:T(8,128)(2,1)} custom-call(s32[32]{0:T(128)} %map_ref.1, bf16[512,256]{1,0:T(8,128)(2,1)} %store_ref.1, bf16[1024,256]{1,0:T(8,128)(2,1)} %ein_ref.1, bf16[512,4096]{1,0:T(8,128)(2,1)} %eout_ref.1, bf16[256,1024]{1,0:T(8,128)(2,1)} %attn_ref.1), custom_call_target="tpu_custom_call" | custom-call | tf_op jit(solution)/shard_map/chain/pallas_call | solution.py:428
  93.3 0.0 copy-done
  93.3 2.0 %add_convert_fusion = bf16[256,1024]{1,0:T(8,128)(2,1)} fusion(bf16[256,1024]{1,0:T(8,128)(2,1)S(1)} %copy-done, bf16[256,1024]{1,0:T(8,128)(2,1)} %chain.1), kind=kLoop, calls=%fused_computation | loop fusion | flops 1048576 | bytes 1572864 | tf_op jit(solution)/shard_map/convert_element_type | solution.py:464
Async XLA Ops:
  0.0 93.3 %copy-start = (bf16[256,1024]{1,0:T(8,128)(2,1)S(1)}, bf16[256,1024]{1,0:T(8,128)(2,1)}, u32[]{:S(2)}) copy-start(bf16[256,1024]{1,0:T(8,128)(2,1)} %param.11) | copy-start | bytes 1572868

commit v4 on v3

--- a/solution.py
+++ b/solution.py
@@ -176,8 +176,6 @@
         zs, ys, b = t // 8, (t // 2) % 4, t % 2
         s = ((zs // 2) * 4 + ys) * 4 + (zs % 2) * 2 + b
         eo[c, pl.ds(pl.multiple_of(t * BLOCK, BLOCK), BLOCK), :] = eo_raw[map_ref[s]].T
-
-    send(eo.at[c], eo.at[c], eo_ss, eo_rs, place(z, xl, oc, xh, y))
 
     attn_near(0)
     send_attn(1)
@@ -228,7 +226,7 @@
         arrived(xr.at[j, hr], x_ss.at[j, hr], x_rs.at[j, hr])
         total = ysum[j, hr] + xr[j, hr].astype(F32)
         a1g[j, h, y] = total.astype(BF16).reshape(4 * rx, 512)
-        for k in (1, 3, 2):
+        for k in (2, 1, 3):
             send(a1g.at[j, h, y], a1g.at[j, h, y], a1_ss.at[j, hr, k], a1_rs.at[j, hr, y],
                  place(z, xl, c, xh, yk(k)))
 
@@ -391,6 +389,7 @@
             if k != 1 or hr != 0:
                 send_partials(1, zk(k), hr)
     relay_store(2, xl, oh)
+    send(eo.at[c], eo.at[c], eo_ss, eo_rs, place(z, xl, oc, xh, y))
     store_arrived()
     multiply_store(0)
     reduce_y(1, 0)
@@ -402,11 +401,11 @@
     relay_x(0)
     multiply_store(1)
     relay_z(0)
+    arrived(eo.at[oc], eo_ss, eo_rs)
+    multiply_out(0)
     reduce_zy()
     spread(1)
-    arrived(eo.at[oc], eo_ss, eo_rs)
     relay_x(1)
-    multiply_out(0)
     relay_z(1)
     relay_out(0, 0)
     relay_out(0, 1)

time: 95.9 us -> 94.2 us (0.982)
  Pallas kernels: 93.3 us -> 91.5 us
    pallas_call x1, Pallas kernels: 93.3 us -> 91.5 us  [shards(): pl.pallas_call(chain_kernel, out_shape=jax.ShapeDtypeStruct((tokens, widt...]
where the time goes in v4:
time: 94.2 us; the launch traced here: 93.5 us
  Pallas kernels  91.5 us (97%)
  other arithmetic  2.03 us (2%)
    pallas_call x1, Pallas kernels, shards(): pl.pallas_call(chain_kernel, out_shape=jax.ShapeDtypeStruct((tokens, widt...  91.5 us
    convert_element_type x1, other arithmetic, shards(): return (products.astype(F32) + residual.astype(F32)).astype(BF16)  2.03 us

profile of v4, /device:TPU:6, one launch (start us, length us, event | category | flops | bytes accessed | tf_op | source)
XLA Modules:
  0.0 93.5 jit_solution(4913260243412540189)
XLA Ops:
  0.0 0.0 copy-start
  0.0 91.5 %chain.1 = bf16[256,1024]{1,0:T(8,128)(2,1)} custom-call(s32[32]{0:T(128)} %map_ref.1, bf16[512,256]{1,0:T(8,128)(2,1)} %store_ref.1, bf16[1024,256]{1,0:T(8,128)(2,1)} %ein_ref.1, bf16[512,4096]{1,0:T(8,128)(2,1)} %eout_ref.1, bf16[256,1024]{1,0:T(8,128)(2,1)} %attn_ref.1), custom_call_target="tpu_custom_call" | custom-call | tf_op jit(solution)/shard_map/chain/pallas_call | solution.py:427
  91.5 0.0 copy-done
  91.5 2.0 %add_convert_fusion = bf16[256,1024]{1,0:T(8,128)(2,1)} fusion(bf16[256,1024]{1,0:T(8,128)(2,1)S(1)} %copy-done, bf16[256,1024]{1,0:T(8,128)(2,1)} %chain.1), kind=kLoop, calls=%fused_computation | loop fusion | flops 1048576 | bytes 1572864 | tf_op jit(solution)/shard_map/convert_element_type | solution.py:463
Async XLA Ops:
  0.0 91.5 %copy-start = (bf16[256,1024]{1,0:T(8,128)(2,1)S(1)}, bf16[256,1024]{1,0:T(8,128)(2,1)}, u32[]{:S(2)}) copy-start(bf16[256,1024]{1,0:T(8,128)(2,1)} %param.11) | copy-start | bytes 1572868

commit v5 on v4

--- a/solution.py
+++ b/solution.py
@@ -56,6 +56,19 @@
     def yk(k):
         return lax.rem(y + k, 4)
 
+    barrier = pltpu.get_barrier_semaphore()
+
+    def greet(target):
+        pl.semaphore_signal(barrier, inc=1, device_id=target, device_id_type=MESH)
+
+    for k in (2, 1, 3):
+        greet(place(zk(k), xl, c, xh, y))
+        greet(place(z, xl, c, xh, yk(k)))
+    greet(place(z, xl, c, oh, y))
+    greet(place(z, ox, c, oh, y))
+    greet(place(z, ox, c, xh, y))
+    greet(place(z, xl, oc, xh, y))
+
     local = [
         pltpu.make_async_copy(attn_ref, attn_g.at[z], loc_sem.at[0]),
         pltpu.make_async_copy(ein_ref.at[:, :128], ein_g.at[q0, 0], loc_sem.at[1]),
@@ -65,29 +78,12 @@
     for copy in local:
         copy.start()
 
-    @pl.loop(0, 32)
-    def _(t):
-        cols = pl.ds(pl.multiple_of(t * BLOCK, BLOCK), BLOCK)
-        pltpu.make_async_copy(eout_ref.at[:, cols], eo_raw.at[t], loc_sem.at[3]).start()
-
-    barrier = pltpu.get_barrier_semaphore()
-
-    def greet(target):
-        pl.semaphore_signal(barrier, inc=1, device_id=target, device_id_type=MESH)
-
-    greet(place(z, xl, oc, xh, y))
-    greet(place(z, ox, c, xh, y))
-    greet(place(z, xl, c, oh, y))
-    greet(place(z, ox, c, oh, y))
-    for k in range(1, 4):
-        greet(place(z, xl, c, xh, yk(k)))
-        greet(place(zk(k), xl, c, xh, y))
     pl.semaphore_wait(barrier, 10)
 
     for a in range(2):
         src = ein_ref.at[:, a * 128:(a + 1) * 128]
+        send(src, ein_g.at[q0, a], ein_ss.at[a, 1], ein_rs.at[q0, a], place(z, ox, c, xh, y))
         send(src, ein_g.at[q0, a], ein_ss.at[a, 0], ein_rs.at[q0, a], place(z, xl, oc, xh, y))
-        send(src, ein_g.at[q0, a], ein_ss.at[a, 1], ein_rs.at[q0, a], place(z, ox, c, xh, y))
 
     def attn_part(zs, j):
         return attn_g.at[zs, pl.ds(j * rows, rows)]
@@ -112,6 +108,11 @@
     mine = s_g.at[q0, xh]
     send(store_ref, mine, s_ss.at[0], s_rs.at[q0, xh], place(z, ox, c, oh, y))
     send(store_ref, mine, s_ss.at[1], s_rs.at[q0, xh], place(z, xl, oc, xh, y))
+
+    @pl.loop(0, 32)
+    def _(t):
+        cols = pl.ds(pl.multiple_of(t * BLOCK, BLOCK), BLOCK)
+        pltpu.make_async_copy(eout_ref.at[:, cols], eo_raw.at[t], loc_sem.at[3]).start()
 
     def half_cols(h):
         return pl.ds(pl.multiple_of(h * 512, 512), 512)
@@ -389,9 +390,9 @@
             if k != 1 or hr != 0:
                 send_partials(1, zk(k), hr)
     relay_store(2, xl, oh)
-    send(eo.at[c], eo.at[c], eo_ss, eo_rs, place(z, xl, oc, xh, y))
     store_arrived()
     multiply_store(0)
+    send(eo.at[c], eo.at[c], eo_ss, eo_rs, place(z, xl, oc, xh, y))
     reduce_y(1, 0)
     reduce_y(1, 1)
     reduce_x(1, 0)

time: 94.2 us -> 94 us (level)
  no operation moved by 1% of the time
where the time goes in v5:
time: 94 us; the launch traced here: 93.6 us
  Pallas kernels  91.6 us (97%)
  other arithmetic  2.03 us (2%)
    pallas_call x1, Pallas kernels, shards(): pl.pallas_call(chain_kernel, out_shape=jax.ShapeDtypeStruct((tokens, widt...  91.6 us
    convert_element_type x1, other arithmetic, shards(): return (products.astype(F32) + residual.astype(F32)).astype(BF16)  2.03 us

profile of v5, /device:TPU:6, one launch (start us, length us, event | category | flops | bytes accessed | tf_op | source)
XLA Modules:
  0.0 93.6 jit_solution(3804477856774645809)
XLA Ops:
  0.0 0.0 copy-start
  0.0 91.6 %chain.1 = bf16[256,1024]{1,0:T(8,128)(2,1)} custom-call(s32[32]{0:T(128)} %map_ref.1, bf16[512,256]{1,0:T(8,128)(2,1)} %store_ref.1, bf16[1024,256]{1,0:T(8,128)(2,1)} %ein_ref.1, bf16[512,4096]{1,0:T(8,128)(2,1)} %eout_ref.1, bf16[256,1024]{1,0:T(8,128)(2,1)} %attn_ref.1), custom_call_target="tpu_custom_call" | custom-call | tf_op jit(solution)/shard_map/chain/pallas_call | solution.py:428
  91.6 0.0 copy-done
  91.6 2.0 %add_convert_fusion = bf16[256,1024]{1,0:T(8,128)(2,1)} fusion(bf16[256,1024]{1,0:T(8,128)(2,1)S(1)} %copy-done, bf16[256,1024]{1,0:T(8,128)(2,1)} %chain.1), kind=kLoop, calls=%fused_computation | loop fusion | flops 1048576 | bytes 1572864 | tf_op jit(solution)/shard_map/convert_element_type | solution.py:464
Async XLA Ops:
  0.0 91.6 %copy-start = (bf16[256,1024]{1,0:T(8,128)(2,1)S(1)}, bf16[256,1024]{1,0:T(8,128)(2,1)}, u32[]{:S(2)}) copy-start(bf16[256,1024]{1,0:T(8,128)(2,1)} %param.11) | copy-start | bytes 1572868

commit v6 on v5

--- a/solution.py
+++ b/solution.py
@@ -62,9 +62,9 @@
         pl.semaphore_signal(barrier, inc=1, device_id=target, device_id_type=MESH)
 
     for k in (2, 1, 3):
-        greet(place(zk(k), xl, c, xh, y))
         greet(place(z, xl, c, xh, yk(k)))
-    greet(place(z, xl, c, oh, y))
+        if k != 2:
+            greet(place(zk(k), xl, c, xh, y))
     greet(place(z, ox, c, oh, y))
     greet(place(z, ox, c, xh, y))
     greet(place(z, xl, oc, xh, y))
@@ -78,7 +78,7 @@
     for copy in local:
         copy.start()
 
-    pl.semaphore_wait(barrier, 10)
+    pl.semaphore_wait(barrier, 8)
 
     for a in range(2):
         src = ein_ref.at[:, a * 128:(a + 1) * 128]

time: 94 us -> 94.3 us (level)
  no operation moved by 1% of the time
where the time goes in v6:
time: 94.3 us; the launch traced here: 93.5 us
  Pallas kernels  91.5 us (97%)
  other arithmetic  2.03 us (2%)
    pallas_call x1, Pallas kernels, shards(): pl.pallas_call(chain_kernel, out_shape=jax.ShapeDtypeStruct((tokens, widt...  91.5 us
    convert_element_type x1, other arithmetic, shards(): return (products.astype(F32) + residual.astype(F32)).astype(BF16)  2.03 us

profile of v6, /device:TPU:6, one launch (start us, length us, event | category | flops | bytes accessed | tf_op | source)
XLA Modules:
  0.0 93.5 jit_solution(5992921980194508741)
XLA Ops:
  0.0 0.0 copy-start
  0.0 91.5 %chain.1 = bf16[256,1024]{1,0:T(8,128)(2,1)} custom-call(s32[32]{0:T(128)} %map_ref.1, bf16[512,256]{1,0:T(8,128)(2,1)} %store_ref.1, bf16[1024,256]{1,0:T(8,128)(2,1)} %ein_ref.1, bf16[512,4096]{1,0:T(8,128)(2,1)} %eout_ref.1, bf16[256,1024]{1,0:T(8,128)(2,1)} %attn_ref.1), custom_call_target="tpu_custom_call" | custom-call | tf_op jit(solution)/shard_map/chain/pallas_call | solution.py:428
  91.5 0.0 copy-done
  91.5 2.0 %add_convert_fusion = bf16[256,1024]{1,0:T(8,128)(2,1)} fusion(bf16[256,1024]{1,0:T(8,128)(2,1)S(1)} %copy-done, bf16[256,1024]{1,0:T(8,128)(2,1)} %chain.1), kind=kLoop, calls=%fused_computation | loop fusion | flops 1048576 | bytes 1572864 | tf_op jit(solution)/shard_map/convert_element_type | solution.py:464
Async XLA Ops:
  0.0 91.5 %copy-start = (bf16[256,1024]{1,0:T(8,128)(2,1)S(1)}, bf16[256,1024]{1,0:T(8,128)(2,1)}, u32[]{:S(2)}) copy-start(bf16[256,1024]{1,0:T(8,128)(2,1)} %param.11) | copy-start | bytes 1572868
